TPU v7x, 32 devices: a whole 2x2x4 slice. The times are simulated.
32 devices in a mesh: row: 2 (over x), col: 8 (over z, y), layer: 2 (over core).
Axes of the slice: x: 2, y: 2, z: 4, core: 2. Of those that a mesh axis runs over, the one named last changes fastest.
Arguments:
- flow: float32 [2048, 2048], P('row', ('col', 'layer')), as said below
- pattern: int32 [4, 4], replicated, may hold values from 0 to 1, as said below
- prune_level: int32 [4], replicated, may hold values from 1 to 8
- power: int32 [4], replicated, may hold values from 1 to 4
Outputs:
- pruned: float32 [2048, 2048], P('row', ('col', 'layer'))
Inputs may be any that keep to these rules, and one draw needn't show every extreme that they name: pattern holds 0 or 1 and its diagonal is all 1; in every draw, all block rows that meet the 1024 rows of one index of row are all 1, and all block columns that meet the columns of one index of col are all 1. flow is positive.
All inputs are finite; a program needn't handle non-finite values.
Results may differ from a plain program's by a relative error of at most 0.00018.
Values sent between devices are 32-bit elements; how exact they have to be, the bound alone decides.
No kernel may reach another device: no remote copies, remote signals or barrier semaphores. Data moves between devices by JAX's collectives and lax.ppermute only.
A program may use at most 128 MiB of HBM per device.

v0:
```python
import jax
import jax.numpy as jnp
from jax import lax
from jax.sharding import PartitionSpec as P


def multiply(left, right):
    exact = lax.Precision.HIGHEST
    return jnp.dot(left, right, precision=exact, preferred_element_type=jnp.float32)


def on_device(flow, pattern, prune_level, power):
    rows, width = flow.shape
    layers = lax.axis_size("layer")
    order = rows * lax.axis_size("row")
    blocks = pattern.shape[0]
    tile_edge = order // blocks
    row_start = lax.axis_index("row") * rows
    col_start = (lax.axis_index("col") * layers + lax.axis_index("layer")) * width
    block_ids = jnp.arange(blocks, dtype=jnp.int32)
    row_ids = (row_start + jnp.arange(rows, dtype=jnp.int32)) // tile_edge
    col_ids = (col_start + jnp.arange(width, dtype=jnp.int32)) // tile_edge
    row_onehot = (row_ids[:, None] == block_ids[None, :]).astype(jnp.float32)
    col_onehot = (block_ids[:, None] == col_ids[None, :]).astype(jnp.float32)
    exact = lax.Precision.HIGHEST
    chosen = jnp.dot(
        jnp.dot(row_onehot, pattern.astype(jnp.float32), precision=exact),
        col_onehot,
        precision=exact,
    )
    masked = flow * chosen
    groups = rows // (layers * width)
    parted = masked.reshape(groups, layers, width, width)
    swapped = lax.all_to_all(parted, "layer", split_axis=1, concat_axis=3, tiled=True)
    inner_rows = swapped.reshape(groups * width, layers * width)
    strip = lax.all_gather(masked, "col", axis=1, tiled=True)
    partial_value = multiply(strip, lax.all_gather(inner_rows, "row", axis=0, tiled=True))
    expanded = lax.psum_scatter(partial_value, "layer", scatter_dimension=1, tiled=True)
    exponents = jnp.dot(power.astype(jnp.float32)[None, :], col_onehot, precision=exact)[0]
    inflated = jnp.power(expanded, exponents[None, :])
    totals = lax.psum(jnp.sum(inflated, axis=0), "row")
    levels = jnp.dot(prune_level.astype(jnp.float32)[None, :], col_onehot, precision=exact)[0] / 8.0
    return jnp.maximum(order * inflated / totals[None, :] - levels[None, :], 0.0)


def solution(mesh):
    return jax.shard_map(
        on_device,
        mesh=mesh,
        in_specs=(P("row", ("col", "layer")), P(), P(), P()),
        out_specs=P("row", ("col", "layer")),
        check_vma=False,
    )
```

profile of v0, /device:TPU:0, one launch (start us, length us, event | category | flops | bytes accessed | tf_op | source)
XLA Modules:
  0.0 145.4 jit_solution(2533182909635452199)
XLA Ops:
  6.5 0.0 all-gather.5.cloned.1.call-start
  6.6 1.1 fusion.1
  7.7 1.7 %convolution_multiply_fusion = f32[1024,128]{1,0:T(8,128)S(1)} fusion(f32[1024,128]{1,0:T(8,128)} %param.4, f32[1024,4]{0,1:T(4,128)S(1)} %fusion.1, s32[128]{0:T(128)S(1)} %and_select_fusion), kind=kOutput, calls=%fused_computation | convolution fusion | flops 6423040 | bytes 1065472 | tf_op jit(solution)/shard_map/dot_general | solution.py:26
  9.4 0.0 copy-start
  9.4 4.2 %all_to_all.15 = f32[4,2,128,128]{3,2,0,1:T(8,128)S(1)} all-to-all(f32[4,2,128,128]{3,2,0,1:T(8,128)S(1)} %copy.6), channel_id=1, replica_groups=mesh['row'=2,'col'=8,'layer'=2] {'layer'}, dimensions={1} | all-to-all | bytes 1048576 | tf_op jit(solution)/shard_map/all_to_all | solution.py:34
  13.6 0.4 copy.7
  14.0 0.9 copy.10
  14.8 0.0 copy-start.1
  14.8 0.0 copy-start.2
  14.9 0.0 all-gather.5.cloned.1.call-update
  14.9 0.0 all-gather.3.cloned.1.call-start
  14.9 0.0 copy-done
  14.9 0.7 all-gather.3.cloned.1.call-update
  15.6 0.0 reduce-scatter.2.cloned.1.call-start
  15.7 23.4 %all-gather.5.cloned.1.call-done = f32[1024,256]{1,0:T(8,128)} async-done(((f32[512,256]{1,0:T(8,128)}), f32[1024,256]{1,0:T(8,128)}) %all-gather.5.cloned.1.call-update) | async-done | bytes 1048592 | tf_op jit(solution)/shard_map/all_gather | solution.py:37
  39.0 77.1 %all-gather.3.cloned.1.call-done = f32[1024,1024]{1,0:T(8,128)} async-done(((f32[1024,128]{1,0:T(8,128)}), f32[1024,1024]{1,0:T(8,128)}) %all-gather.3.cloned.1.call-update) | async-done | bytes 4194320 | tf_op jit(solution)/shard_map/all_gather | solution.py:36
  116.1 6.9 %fusion.10 = f32[1024,256]{1,0:T(8,128)} fusion(f32[1024,1024]{1,0:T(8,128)} %all-gather.3.cloned.1.call-done, f32[1024,256]{1,0:T(8,128)} %all-gather.5.cloned.1.call-done), kind=kOutput, calls=%fused_computation.30 | convolution fusion | flops 3221225472 | bytes 6291456 | tf_op jit(solution)/shard_map/dot_general | solution.py:9
  123.0 0.0 reduce-scatter.2.cloned.1.call-update
  123.1 0.0 copy-done.1
  123.1 0.1 convolution_bitcast_fusion.1
  123.2 0.0 copy-done.2
  123.2 0.1 fusion
  123.3 6.6 %reduce-scatter.2.cloned.1.call-done = f32[1024,128]{1,0:T(8,128)} async-done(((f32[1024,256]{1,0:T(8,128)}), f32[1024,128]{1,0:T(8,128)}) %reduce-scatter.2.cloned.1.call-update) | async-done | bytes 524304 | tf_op jit(solution)/shard_map/reduce_scatter | solution.py:38
  129.9 1.6 %power_reduce_fusion = f32[128]{0:T(128)S(1)} fusion(f32[1024,128]{1,0:T(8,128)} %reduce-scatter.2.cloned.1.call-done, f32[128]{0:T(128)S(1)} %convolution_bitcast_fusion.1), kind=kLoop, calls=%fused_computation.8 | loop fusion | flops 130944 | bytes 525312 | tf_op jit(solution)/shard_map/reduce_sum | solution.py:41
  131.5 4.9 %psum.7 = f32[128]{0:T(128)S(1)} all-reduce(f32[128]{0:T(128)S(1)} %power_reduce_fusion), channel_id=1, replica_groups=mesh['row'=2,'col'=8,'layer'=2] {'row'}, use_global_device_ids=true, to_apply=%region_2.3 | all-reduce | flops 128 | bytes 1024 | tf_op jit(solution)/shard_map/psum | solution.py:41
  136.5 2.4 %subtract_maximum_fusion = f32[1024,128]{1,0:T(8,128)} fusion(f32[1024,128]{1,0:T(8,128)} %reduce-scatter.2.cloned.1.call-done, f32[128]{0:T(128)S(1)} %fusion, f32[128]{0:T(128)S(1)} %psum.7, f32[128]{0:T(128)S(1)} %convolution_bitcast_fusion.1), kind=kLoop, calls=%fused_computation.5 | loop fusion | flops 524288 | bytes 1050112 | tf_op jit(solution)/shard_map/max | solution.py:43
  (3 shorter events, 0.1 us)
Async XLA Ops:
  6.5 32.5 %all-gather.5.cloned.1.call-start = ((), (), s32[]{:S(2)}) async-start(), calls=%async_computation.3 | async-start | bytes 1572864 | tf_op jit(solution)/shard_map/all_gather | solution.py:37
  9.4 5.6 %copy-start = (f32[1024,128]{1,0:T(8,128)}, f32[1024,128]{1,0:T(8,128)S(1)}, u32[]{:S(2)}) copy-start(f32[1024,128]{1,0:T(8,128)S(1)} %convolution_multiply_fusion) | copy-start | bytes 1572868
  14.8 108.2 %copy-start.1 = (s32[4]{0:T(128)S(1)}, s32[4]{0:T(128)}, u32[]{:S(2)}) copy-start(s32[4]{0:T(128)} %param.7) | copy-start | bytes 52
  14.8 108.3 %copy-start.2 = (s32[4]{0:T(128)S(1)}, s32[4]{0:T(128)}, u32[]{:S(2)}) copy-start(s32[4]{0:T(128)} %param.6) | copy-start | bytes 52
  14.9 101.3 %all-gather.3.cloned.1.call-start = ((), (), s32[]{:S(2)}) async-start(), calls=%async_computation.2 | async-start | bytes 4718592 | tf_op jit(solution)/shard_map/all_gather | solution.py:36
  15.6 114.3 %reduce-scatter.2.cloned.1.call-start = ((), (), s32[]{:S(2)}) async-start(), calls=%async_computation.4 | async-start | bytes 1572864 | tf_op jit(solution)/shard_map/reduce_scatter | solution.py:38
Sparse Core Ops, SparseCore 0:
  15.0 23.9 all-gather.4
  41.1 75.0 all-gather.2
  123.2 6.7 reduce-scatter.1
where the time goes:
time: 146 us; the launch traced here: 145 us
  waiting for transfers between devices  108 us (74%)
  between operations  13.2 us (9%)
  matrix products  9.94 us (7%)
  blocking collectives  9.09 us (6%)
  other arithmetic  4.05 us (3%)
    all_gather x1, waiting for transfers between devices, on_device(): strip = lax.all_gather(masked, 'col', axis=1, tiled=True)  77.1 us
    all_gather x1, waiting for transfers between devices, on_device(): lax.all_gather(inner_rows, 'row', axis=0, tiled=True)  23.4 us
    dot_general x1, matrix products, multiply(): jnp.dot(left, right, precision=exact, preferred_element_type=jnp.float32)  6.9 us
    reduce_scatter x1, waiting for transfers between devices, on_device(): lax.psum_scatter(partial_value, 'layer', scatter_dimension=1, tiled=True)  6.61 us
    psum x1, blocking collectives, on_device(): totals = lax.psum(jnp.sum(inflated, axis=0), 'row')  4.94 us
    all_to_all x1, blocking collectives, on_device(): lax.all_to_all(parted, 'layer', split_axis=1, concat_axis=3, tiled=True)  4.15 us
  transfers between devices with their start and end apart: 3, of which 3 were waited for; matrix products, arithmetic and copies ran while one was open for 0% of the time, Pallas kernels for 0%

commit v1 on v0

--- a/solution.py
+++ b/solution.py
@@ -38,7 +38,9 @@
     expanded = lax.psum_scatter(partial_value, "layer", scatter_dimension=1, tiled=True)
     exponents = jnp.dot(power.astype(jnp.float32)[None, :], col_onehot, precision=exact)[0]
     inflated = jnp.power(expanded, exponents[None, :])
-    totals = lax.psum(jnp.sum(inflated, axis=0), "row")
+    x = jnp.sum(inflated, axis=0)
+    shards = lax.all_gather(x, "row")
+    totals = jnp.sum(shards, axis=0)
     levels = jnp.dot(prune_level.astype(jnp.float32)[None, :], col_onehot, precision=exact)[0] / 8.0
     return jnp.maximum(order * inflated / totals[None, :] - levels[None, :], 0.0)
 

time: 146 us -> 145 us (level)
    psum x1 -> x0, blocking collectives: 4.94 us -> none  [on_device(): totals = lax.psum(jnp.sum(inflated, axis=0), 'row')]
    all_gather x0 -> x1, blocking collectives: none -> 4.21 us  [on_device(): shards = lax.all_gather(x, 'row')]
where the time goes in v1:
time: 145 us
  waiting for transfers between devices  108 us (74%)
  between operations  13.2 us (9%)
  matrix products  9.94 us (7%)
  blocking collectives  8.37 us (6%)
  other arithmetic  4.07 us (3%)
    all_gather x1, waiting for transfers between devices, on_device(): strip = lax.all_gather(masked, 'col', axis=1, tiled=True)  77.1 us
    all_gather x1, waiting for transfers between devices, on_device(): lax.all_gather(inner_rows, 'row', axis=0, tiled=True)  23.4 us
    dot_general x1, matrix products, multiply(): jnp.dot(left, right, precision=exact, preferred_element_type=jnp.float32)  6.9 us
    reduce_scatter x1, waiting for transfers between devices, on_device(): lax.psum_scatter(partial_value, 'layer', scatter_dimension=1, tiled=True)  6.61 us
    all_gather x1, blocking collectives, on_device(): shards = lax.all_gather(x, 'row')  4.21 us
    all_to_all x1, blocking collectives, on_device(): lax.all_to_all(parted, 'layer', split_axis=1, concat_axis=3, tiled=True)  4.15 us
  transfers between devices with their start and end apart: 3, of which 3 were waited for; matrix products, arithmetic and copies ran while one was open for 0% of the time, Pallas kernels for 0%

profile of v1, /device:TPU:0, one launch (start us, length us, event | category | flops | bytes accessed | tf_op | source)
XLA Modules:
  0.0 144.7 jit_solution(5760475188110092855)
XLA Ops:
  6.5 0.0 all-gather.7.cloned.1.call-start
  6.6 1.1 fusion.1
  7.7 1.7 %convolution_multiply_fusion = f32[1024,128]{1,0:T(8,128)S(1)} fusion(f32[1024,128]{1,0:T(8,128)} %param.4, f32[1024,4]{0,1:T(4,128)S(1)} %fusion.1, s32[128]{0:T(128)S(1)} %and_select_fusion), kind=kOutput, calls=%fused_computation | convolution fusion | flops 6423040 | bytes 1065472 | tf_op jit(solution)/shard_map/dot_general | solution.py:26
  9.4 0.0 copy-start
  9.4 4.2 %all_to_all.15 = f32[4,2,128,128]{3,2,0,1:T(8,128)S(1)} all-to-all(f32[4,2,128,128]{3,2,0,1:T(8,128)S(1)} %copy.6), channel_id=1, replica_groups=mesh['row'=2,'col'=8,'layer'=2] {'layer'}, dimensions={1} | all-to-all | bytes 1048576 | tf_op jit(solution)/shard_map/all_to_all | solution.py:34
  13.6 0.4 copy.7
  14.0 0.9 copy.10
  14.8 0.0 copy-start.1
  14.8 0.0 copy-start.2
  14.9 0.0 all-gather.7.cloned.1.call-update
  14.9 0.0 all-gather.5.cloned.1.call-start
  14.9 0.0 copy-done
  14.9 0.7 all-gather.5.cloned.1.call-update
  15.6 0.0 reduce-scatter.2.cloned.1.call-start
  15.7 23.4 %all-gather.7.cloned.1.call-done = f32[1024,256]{1,0:T(8,128)} async-done(((f32[512,256]{1,0:T(8,128)}), f32[1024,256]{1,0:T(8,128)}) %all-gather.7.cloned.1.call-update) | async-done | bytes 1048592 | tf_op jit(solution)/shard_map/all_gather | solution.py:37
  39.0 77.1 %all-gather.5.cloned.1.call-done = f32[1024,1024]{1,0:T(8,128)} async-done(((f32[1024,128]{1,0:T(8,128)}), f32[1024,1024]{1,0:T(8,128)}) %all-gather.5.cloned.1.call-update) | async-done | bytes 4194320 | tf_op jit(solution)/shard_map/all_gather | solution.py:36
  116.1 6.9 %fusion.10 = f32[1024,256]{1,0:T(8,128)} fusion(f32[1024,1024]{1,0:T(8,128)} %all-gather.5.cloned.1.call-done, f32[1024,256]{1,0:T(8,128)} %all-gather.7.cloned.1.call-done), kind=kOutput, calls=%fused_computation.30 | convolution fusion | flops 3221225472 | bytes 6291456 | tf_op jit(solution)/shard_map/dot_general | solution.py:9
  123.0 0.0 reduce-scatter.2.cloned.1.call-update
  123.1 0.0 copy-done.1
  123.1 0.1 convolution_bitcast_fusion.1
  123.2 0.0 copy-done.2
  123.2 0.1 fusion
  123.3 6.6 %reduce-scatter.2.cloned.1.call-done = f32[1024,128]{1,0:T(8,128)} async-done(((f32[1024,256]{1,0:T(8,128)}), f32[1024,128]{1,0:T(8,128)}) %reduce-scatter.2.cloned.1.call-update) | async-done | bytes 524304 | tf_op jit(solution)/shard_map/reduce_scatter | solution.py:38
  129.9 1.6 %power_reduce_fusion = f32[128]{0:T(128)S(1)} fusion(f32[1024,128]{1,0:T(8,128)} %reduce-scatter.2.cloned.1.call-done, f32[128]{0:T(128)S(1)} %convolution_bitcast_fusion.1), kind=kLoop, calls=%fused_computation.8 | loop fusion | flops 130944 | bytes 525312 | tf_op jit(solution)/shard_map/reduce_sum | solution.py:41
  131.5 4.2 %all-gather.1 = f32[2,1,128]{2,1,0:T(1,128)S(1)} all-gather(f32[1,1,128]{2,1,0:T(1,128)S(1)} %bitcast.30), channel_id=2, replica_groups=mesh['row'=2,'col'=8,'layer'=2] {'row'}, dimensions={0}, use_global_device_ids=true | all-gather | bytes 1536 | tf_op jit(solution)/shard_map/all_gather | solution.py:42
  135.8 2.4 %subtract_maximum_fusion = f32[1024,128]{1,0:T(8,128)} fusion(f32[1024,128]{1,0:T(8,128)} %reduce-scatter.2.cloned.1.call-done, f32[128]{0:T(128)S(1)} %fusion, f32[128]{0:T(128)S(1)} %reduce_sum.19, f32[128]{0:T(128)S(1)} %convolution_bitcast_fusion.1), kind=kLoop, calls=%fused_computation.5 | loop fusion | flops 524288 | bytes 1050112 | tf_op jit(solution)/shard_map/max | solution.py:45
  (4 shorter events, 0.1 us)
Async XLA Ops:
  6.5 32.5 %all-gather.7.cloned.1.call-start = ((), (), s32[]{:S(2)}) async-start(), calls=%async_computation.3 | async-start | bytes 1572864 | tf_op jit(solution)/shard_map/all_gather | solution.py:37
  9.4 5.6 %copy-start = (f32[1024,128]{1,0:T(8,128)}, f32[1024,128]{1,0:T(8,128)S(1)}, u32[]{:S(2)}) copy-start(f32[1024,128]{1,0:T(8,128)S(1)} %convolution_multiply_fusion) | copy-start | bytes 1572868
  14.8 108.2 %copy-start.1 = (s32[4]{0:T(128)S(1)}, s32[4]{0:T(128)}, u32[]{:S(2)}) copy-start(s32[4]{0:T(128)} %param.7) | copy-start | bytes 52
  14.8 108.3 %copy-start.2 = (s32[4]{0:T(128)S(1)}, s32[4]{0:T(128)}, u32[]{:S(2)}) copy-start(s32[4]{0:T(128)} %param.6) | copy-start | bytes 52
  14.9 101.3 %all-gather.5.cloned.1.call-start = ((), (), s32[]{:S(2)}) async-start(), calls=%async_computation.2 | async-start | bytes 4718592 | tf_op jit(solution)/shard_map/all_gather | solution.py:36
  15.6 114.3 %reduce-scatter.2.cloned.1.call-start = ((), (), s32[]{:S(2)}) async-start(), calls=%async_computation.4 | async-start | bytes 1572864 | tf_op jit(solution)/shard_map/reduce_scatter | solution.py:38
Sparse Core Ops, SparseCore 0:
  15.0 23.9 all-gather.6
  41.1 75.0 all-gather.4
  123.2 6.7 reduce-scatter.1

commit v2 on v0

--- a/solution.py
+++ b/solution.py
@@ -31,7 +31,10 @@
     masked = flow * chosen
     groups = rows // (layers * width)
     parted = masked.reshape(groups, layers, width, width)
-    swapped = lax.all_to_all(parted, "layer", split_axis=1, concat_axis=3, tiled=True)
+    size = lax.axis_size("layer")
+    pieces = jnp.stack(jnp.split(parted, size, axis=1), axis=0)
+    pieces = lax.all_to_all(pieces, "layer", split_axis=0, concat_axis=0)
+    swapped = jnp.concatenate(pieces, axis=3)
     inner_rows = swapped.reshape(groups * width, layers * width)
     strip = lax.all_gather(masked, "col", axis=1, tiled=True)
     partial_value = multiply(strip, lax.all_gather(inner_rows, "row", axis=0, tiled=True))

time: 146 us -> 146 us (level)
  no operation moved by 1% of the time
where the time goes in v2:
time: 146 us; the launch traced here: 145 us
  waiting for transfers between devices  108 us (74%)
  between operations  13.2 us (9%)
  matrix products  9.95 us (7%)
  blocking collectives  9.09 us (6%)
  other arithmetic  4.09 us (3%)
    all_gather x1, waiting for transfers between devices, on_device(): strip = lax.all_gather(masked, 'col', axis=1, tiled=True)  77.1 us
    all_gather x1, waiting for transfers between devices, on_device(): lax.all_gather(inner_rows, 'row', axis=0, tiled=True)  23.4 us
    dot_general x1, matrix products, multiply(): jnp.dot(left, right, precision=exact, preferred_element_type=jnp.float32)  6.91 us
    reduce_scatter x1, waiting for transfers between devices, on_device(): lax.psum_scatter(partial_value, 'layer', scatter_dimension=1, tiled=True)  6.64 us
    psum x1, blocking collectives, on_device(): totals = lax.psum(jnp.sum(inflated, axis=0), 'row')  4.94 us
    all_to_all x1, blocking collectives, on_device(): pieces = lax.all_to_all(pieces, 'layer', split_axis=0, concat_axis=0)  4.15 us
  transfers between devices with their start and end apart: 3, of which 3 were waited for; matrix products, arithmetic and copies ran while one was open for 0% of the time, Pallas kernels for 0%

profile of v2, /device:TPU:0, one launch (start us, length us, event | category | flops | bytes accessed | tf_op | source)
XLA Modules:
  0.0 145.5 jit_solution(1314343911504710024)
XLA Ops:
  6.5 0.0 all-gather.5.cloned.1.call-start
  6.6 1.1 fusion.1
  7.7 1.7 %convolution_multiply_fusion = f32[1024,128]{1,0:T(8,128)S(1)} fusion(f32[1024,128]{1,0:T(8,128)} %param.4, f32[1024,4]{0,1:T(4,128)S(1)} %fusion.1, s32[128]{0:T(128)S(1)} %and_select_fusion), kind=kOutput, calls=%fused_computation | convolution fusion | flops 6423040 | bytes 1065472 | tf_op jit(solution)/shard_map/dot_general | solution.py:26
  9.4 0.0 copy-start
  9.5 4.2 %all_to_all.5 = f32[2,4,1,128,128]{4,3,1,2,0:T(8,128)S(1)} all-to-all(f32[2,4,1,128,128]{4,3,1,2,0:T(8,128)S(1)} %pad_maximum_fusion), channel_id=1, replica_groups=mesh['row'=2,'col'=8,'layer'=2] {'layer'}, dimensions={0} | all-to-all | bytes 1048576 | tf_op jit(solution)/shard_map/all_to_all | solution.py:36
  13.6 0.4 copy.10
  14.0 0.8 copy.15
  14.9 0.0 copy-start.1
  14.9 0.0 copy-start.2
  14.9 0.0 all-gather.5.cloned.1.call-update
  14.9 0.0 all-gather.3.cloned.1.call-start
  15.0 0.0 copy-done
  15.0 0.7 all-gather.3.cloned.1.call-update
  15.7 0.0 reduce-scatter.2.cloned.1.call-start
  15.7 23.4 %all-gather.5.cloned.1.call-done = f32[1024,256]{1,0:T(8,128)} async-done(((f32[512,256]{1,0:T(8,128)}), f32[1024,256]{1,0:T(8,128)}) %all-gather.5.cloned.1.call-update) | async-done | bytes 1048592 | tf_op jit(solution)/shard_map/all_gather | solution.py:40
  39.1 77.1 %all-gather.3.cloned.1.call-done = f32[1024,1024]{1,0:T(8,128)} async-done(((f32[1024,128]{1,0:T(8,128)}), f32[1024,1024]{1,0:T(8,128)}) %all-gather.3.cloned.1.call-update) | async-done | bytes 4194320 | tf_op jit(solution)/shard_map/all_gather | solution.py:39
  116.2 6.9 %fusion.10 = f32[1024,256]{1,0:T(8,128)} fusion(f32[1024,1024]{1,0:T(8,128)} %all-gather.3.cloned.1.call-done, f32[1024,256]{1,0:T(8,128)} %all-gather.5.cloned.1.call-done), kind=kOutput, calls=%fused_computation.33 | convolution fusion | flops 3221225472 | bytes 6291456 | tf_op jit(solution)/shard_map/dot_general | solution.py:9
  123.1 0.0 reduce-scatter.2.cloned.1.call-update
  123.1 0.0 copy-done.1
  123.1 0.1 convolution_bitcast_fusion.1
  123.2 0.0 copy-done.2
  123.2 0.1 fusion
  123.4 6.6 %reduce-scatter.2.cloned.1.call-done = f32[1024,128]{1,0:T(8,128)} async-done(((f32[1024,256]{1,0:T(8,128)}), f32[1024,128]{1,0:T(8,128)}) %reduce-scatter.2.cloned.1.call-update) | async-done | bytes 524304 | tf_op jit(solution)/shard_map/reduce_scatter | solution.py:41
  130.0 1.6 %power_reduce_fusion = f32[128]{0:T(128)S(1)} fusion(f32[1024,128]{1,0:T(8,128)} %reduce-scatter.2.cloned.1.call-done, f32[128]{0:T(128)S(1)} %convolution_bitcast_fusion.1), kind=kLoop, calls=%fused_computation.9 | loop fusion | flops 130944 | bytes 525312 | tf_op jit(solution)/shard_map/reduce_sum | solution.py:44
  131.6 4.9 %psum.7 = f32[128]{0:T(128)S(1)} all-reduce(f32[128]{0:T(128)S(1)} %power_reduce_fusion), channel_id=1, replica_groups=mesh['row'=2,'col'=8,'layer'=2] {'row'}, use_global_device_ids=true, to_apply=%region_2.3 | all-reduce | flops 128 | bytes 1024 | tf_op jit(solution)/shard_map/psum | solution.py:44
  136.5 2.4 %subtract_maximum_fusion = f32[1024,128]{1,0:T(8,128)} fusion(f32[1024,128]{1,0:T(8,128)} %reduce-scatter.2.cloned.1.call-done, f32[128]{0:T(128)S(1)} %fusion, f32[128]{0:T(128)S(1)} %psum.7, f32[128]{0:T(128)S(1)} %convolution_bitcast_fusion.1), kind=kLoop, calls=%fused_computation.6 | loop fusion | flops 524288 | bytes 1050112 | tf_op jit(solution)/shard_map/max | solution.py:46
  (4 shorter events, 0.1 us)
Async XLA Ops:
  6.5 32.5 %all-gather.5.cloned.1.call-start = ((), (), s32[]{:S(2)}) async-start(), calls=%async_computation.3 | async-start | bytes 1572864 | tf_op jit(solution)/shard_map/all_gather | solution.py:40
  9.4 5.6 %copy-start = (f32[1024,128]{1,0:T(8,128)}, f32[1024,128]{1,0:T(8,128)S(1)}, u32[]{:S(2)}) copy-start(f32[1024,128]{1,0:T(8,128)S(1)} %convolution_multiply_fusion) | copy-start | bytes 1572868
  14.9 108.2 %copy-start.1 = (s32[4]{0:T(128)S(1)}, s32[4]{0:T(128)}, u32[]{:S(2)}) copy-start(s32[4]{0:T(128)} %param.7) | copy-start | bytes 52
  14.9 108.3 %copy-start.2 = (s32[4]{0:T(128)S(1)}, s32[4]{0:T(128)}, u32[]{:S(2)}) copy-start(s32[4]{0:T(128)} %param.6) | copy-start | bytes 52
  14.9 101.3 %all-gather.3.cloned.1.call-start = ((), (), s32[]{:S(2)}) async-start(), calls=%async_computation.2 | async-start | bytes 4718592 | tf_op jit(solution)/shard_map/all_gather | solution.py:39
  15.7 114.3 %reduce-scatter.2.cloned.1.call-start = ((), (), s32[]{:S(2)}) async-start(), calls=%async_computation.4 | async-start | bytes 1572864 | tf_op jit(solution)/shard_map/reduce_scatter | solution.py:41
Sparse Core Ops, SparseCore 0:
  15.0 23.9 all-gather.4
  41.1 75.0 all-gather.2
  123.2 6.7 reduce-scatter.1
